TPU v7x, 32 devices: a whole 2x2x4 slice. The times are simulated.
32 devices in a mesh: rows: 8 (over y, x, core), mlp: 4 (over z).
Axes of the slice: x: 2, y: 2, z: 4, core: 2. Of those that a mesh axis runs over, the one named last changes fastest.
Arguments:
- images: bfloat16 [64, 197, 768], P(('rows', 'mlp')), may hold values from -6 to 6
- patch_rank: int32 [64, 197], P(('rows', 'mlp')), may hold values from 0 to 196, each once within a row
- kept_count: int32 [64], P(('rows', 'mlp')), may hold values from 98 to 197
- ln1_gain: float32 [768], replicated, may hold values from 0.1 to 1.9
- router_weight: bfloat16 [768], replicated, may hold values from -0.21875 to 0.21875
- w_qkv: bfloat16 [768, 2304], replicated, may hold values from -0.21875 to 0.21875
- w_out: bfloat16 [768, 768], replicated, may hold values from -2.5 to 2.5
- ln2_gain: float32 [768], replicated, may hold values from 0.1 to 1.9
- w_fc1: bfloat16 [768, 3072], P(None, 'mlp'), may hold values from -0.21875 to 0.21875
- w_fc2: bfloat16 [3072, 768], P('mlp'), may hold values from -0.109375 to 0.109375
- cotangent: bfloat16 [64, 197, 768], P(('rows', 'mlp')), may hold values from -6 to 6
Outputs:
- block_out: bfloat16 [64, 197, 768], P(('rows', 'mlp'))
- grad_images: bfloat16 [64, 197, 768], P(('rows', 'mlp'))
- grad_ln1_gain: float32 [768], replicated
- grad_router: float32 [768], replicated
- grad_qkv: float32 [768, 2304], replicated
- grad_out: float32 [768, 768], replicated
- grad_ln2_gain: float32 [768], replicated
- grad_fc1: float32 [768, 3072], P(None, 'mlp')
- grad_fc2: float32 [3072, 768], P('mlp')
All inputs are finite; a program needn't handle non-finite values.
Results may differ from a plain program's by a relative error of at most 0.012.
The roundings to bfloat16 on the way count: a program that leaves them out, or rounds other values in their place, can miss the bound.
Values may be sent and summed in bfloat16 or wider, within the bound.
A program may use at most 128 MiB of HBM per device.

v0:
```python
import functools
import jax
import jax.numpy as jnp
from jax import lax
from jax.experimental import pallas as pl
from jax.experimental.pallas import tpu as pltpu
from jax.sharding import PartitionSpec as P

HEADS = 12
EPS = 1e-6
FILL = -1e30
BF = jnp.bfloat16
F32 = jnp.float32


def dot_nn(a, b):
    return lax.dot_general(a, b, (((1,), (0,)), ((), ())), preferred_element_type=F32)


def dot_nt(a, b):
    return lax.dot_general(a, b, (((1,), (1,)), ((), ())), preferred_element_type=F32)


def dot_tn(a, b):
    return lax.dot_general(a, b, (((0,), (0,)), ((), ())), preferred_element_type=F32)


def unit_rows(v):
    center = v - jnp.mean(v, -1, keepdims=True)
    scale = lax.rsqrt(jnp.mean(center * center, -1, keepdims=True) + EPS)
    return center * scale, scale


def norm_pull(dy, gain, unit, scale):
    du = dy * gain
    return scale * (
        du
        - jnp.mean(du, -1, keepdims=True)
        - unit * jnp.mean(du * unit, -1, keepdims=True)
    )


def half_mask(rows, h):
    lane = lax.broadcasted_iota(jnp.int32, (rows, 128), 1)
    return (lane < 64) if h == 0 else (lane >= 64)


def forward_rows(i, x_ref, rank_ref, kept_ref, g1_ref, rw_ref, xp, keep, gate, h1, work):
    patches = x_ref.shape[0]
    tall = xp.shape[0] // x_ref.shape[1]
    rows = pl.ds(pl.multiple_of(i * tall, 16), tall)
    work[...] = jnp.zeros_like(work)
    work[0:patches, :] = x_ref[:, i, :]
    v = work[...]
    xp[rows, :] = v
    kept = (rank_ref[pl.ds(i, 1), :] < kept_ref[i]).astype(F32)
    keep_row = jnp.concatenate([kept, jnp.zeros((1, 256 - patches), F32)], 1)
    keep_col = jnp.broadcast_to(keep_row, (128, 256)).T
    keep[rows, :] = keep_col[0:tall, :]
    unit, _ = unit_rows(v.astype(F32))
    low = (unit * g1_ref[...][None]).astype(BF)
    h1[rows, :] = low
    logit = jnp.sum(low.astype(F32) * rw_ref[...][None].astype(F32), -1, keepdims=True)
    gate[rows, :] = jnp.broadcast_to(jax.nn.sigmoid(logit), (tall, 128))


def forward_qkv(j, h1, wqkv, qkv):
    cols = pl.ds(pl.multiple_of(j * 256, 256), 256)
    qkv[:, cols] = dot_nn(h1[...], wqkv[:, cols]).astype(BF)


def attend(p, i, width, tall, qkv, keep, probs, context, contextt):
    rows = pl.ds(pl.multiple_of(i * tall, 16), tall)
    qc = pl.ds(pl.multiple_of(p * 128, 128), 128)
    kc = pl.ds(pl.multiple_of(width + p * 128, 128), 128)
    vc = pl.ds(pl.multiple_of(2 * width + p * 128, 128), 128)
    q, k, v = qkv[rows, qc], qkv[rows, kc], qkv[rows, vc]
    vt = v.T
    kept = keep[rows, 0:1] > 0.5
    outs = []
    for h in range(2):
        kh = jnp.where(half_mask(tall, h), k, jnp.zeros_like(k))
        s = jnp.where(kept, dot_nt(kh, q) * 0.125, FILL)
        e = jnp.exp(s - jnp.max(s, 0, keepdims=True))
        pr = e * (1.0 / jnp.sum(e, 0, keepdims=True))
        probs[i, p * 2 + h] = pr
        outs.append(dot_nn(vt[h * 64 : h * 64 + 64, :], pr.astype(BF)))
    ct = jnp.concatenate(outs, 0)
    contextt[i, pl.ds(pl.multiple_of(p * 128, 128), 128), :] = ct.astype(BF)
    context[rows, qc] = ct.T.astype(BF)


def forward_out(i, tall, context, wout, xp, keep, gate, g2_ref, attended, middle, h2):
    rows = pl.ds(pl.multiple_of(i * tall, 16), tall)
    att = dot_nn(context[rows, :], wout[...])
    attended[rows, :] = att
    mid = xp[rows, :].astype(F32) + keep[rows, 0:1] * gate[rows, 0:1] * att
    middle[rows, :] = mid
    unit, _ = unit_rows(mid)
    h2[rows, :] = (unit * g2_ref[...][None]).astype(BF)


def gelu_pair(pre):
    cdf = 0.5 * (1.0 + lax.erf(pre * 0.7071067811865476))
    pdf = jnp.exp(pre * pre * -0.5) * 0.3989422804014327
    return pre * cdf, cdf + pre * pdf


def mlp_rows(h, c, w1, w2):
    pre = dot_nn(h, w1)
    hidden, slope = gelu_pair(pre)
    grad = dot_nt(c, w2) * slope
    return hidden.astype(BF), grad.astype(BF)


def back_rows(i, tall, c_ref, gh2, middle, keep, gate, attended, g2_ref, gmid, gatt, glogit, dg2):
    rows = pl.ds(pl.multiple_of(i * tall, 16), tall)
    dy = gh2[rows, :]
    unit, scale = unit_rows(middle[rows, :])
    gm = c_ref[rows, :].astype(F32) + norm_pull(dy, g2_ref[...][None], unit, scale)
    gmid[rows, :] = gm
    dg2[...] += jnp.sum(dy * unit, 0, keepdims=True)
    k, g = keep[rows, 0:1], gate[rows, 0:1]
    kept = gm * k
    gatt[rows, :] = (kept * g).astype(BF)
    gl = jnp.sum(kept * attended[rows, :], -1, keepdims=True) * g * (1.0 - g)
    glogit[rows, :] = jnp.broadcast_to(gl, (tall, 128))


def attend_back(p, i, width, tall, qkv, probs, gctx):
    rows = pl.ds(pl.multiple_of(i * tall, 16), tall)
    qc = pl.ds(pl.multiple_of(p * 128, 128), 128)
    kc = pl.ds(pl.multiple_of(width + p * 128, 128), 128)
    vc = pl.ds(pl.multiple_of(2 * width + p * 128, 128), 128)
    q, k, v = qkv[rows, qc], qkv[rows, kc], qkv[rows, vc]
    gc = gctx[rows, qc]
    kt = k.T
    gv, gk, gq = 0.0, 0.0, []
    for h in range(2):
        mask = half_mask(tall, h)
        zero = jnp.zeros_like(v)
        pr = probs[i, p * 2 + h]
        gp = dot_nt(jnp.where(mask, v, zero), gc)
        gs = (pr * (gp - jnp.sum(pr * gp, 0, keepdims=True))).astype(BF)
        gv = gv + dot_nn(pr.astype(BF), jnp.where(mask, gc, zero))
        gk = gk + dot_nn(gs, jnp.where(mask, q, zero))
        gq.append(dot_nn(kt[h * 64 : h * 64 + 64, :], gs))
    qkv[rows, qc] = (jnp.concatenate(gq, 0).T * 0.125).astype(BF)
    qkv[rows, kc] = (gk * 0.125).astype(BF)
    qkv[rows, vc] = gv.astype(BF)


def pair_columns(wqkv, p, width):
    return jnp.concatenate(
        [wqkv[:, pl.ds(pl.multiple_of(b * width + p * 128, 128), 128)] for b in range(3)], 1
    )


def back_input(i, tall, dy, glogit, rw_ref, xp, h1, g1_ref, gmid, gx_ref, dg1, drw):
    rows = pl.ds(pl.multiple_of(i * tall, 16), tall)
    patches = gx_ref.shape[0]
    gl = glogit[rows, 0:1]
    dy = dy + gl * rw_ref[...][None].astype(F32)
    unit, scale = unit_rows(xp[rows, :].astype(F32))
    dg1[...] += jnp.sum(dy * unit, 0, keepdims=True)
    drw[...] += jnp.sum(h1[rows, :].astype(F32) * gl, 0, keepdims=True)
    out = gmid[rows, :] + norm_pull(dy, g1_ref[...][None], unit, scale)
    gx_ref[:, i, :] = out.astype(BF)[0:patches, :]

MESH = pl.DeviceIdType.MESH
CHUNKS = HEADS // 2 + 2
WIDEN = 8
PATHS = ("xzy", "zxy", "yzx", "xzy", "yxz", "xyz", "yzx", "yzx")
ORDER = (
    "osend", "back0", "pairs0", "back1", "pairs1", "fa10", "fa11", "last0", "pairs2", "last1", "fa01", "c2.1",
    "pairs3", "fb1", "c4.1", "last2", "c5.1", "out1", "c3.1", "c2.2", "fa00", "out0", "finish0", "c6.1", "c1.1",
    "c4.2", "c0.1", "c5.2", "finish1", "c3.2", "c7.1", "c6.2", "c2.3", "c1.2", "fb0", "c5.3", "fc", "c0.2", "c4.3",
    "c5.4", "g1", "c1.3", "c6.3", "c2.4", "c3.3", "c7.2", "c0.3", "c4.4", "fd", "c1.4", "c5.5", "c0.4", "c4.5",
    "c6.4", "c7.3", "c3.4", "c5.6", "g2", "c2.5", "c0.5", "c4.6", "c7.4", "c6.5", "fe", "c1.5", "c2.6", "c5.7",
    "c3.5", "c4.7", "c0.6", "g3", "c6.6", "c7.5", "c3.6", "c2.7", "c1.6", "c0.7", "c7.6", "c5.8", "ff", "c6.7",
    "c4.8", "o0", "c1.7", "g4", "c3.7", "c2.8", "c7.7", "c0.8", "c4.9", "c6.8", "c1.8", "c3.8", "c7.8", "c0.9",
    "c5.9", "c1.9", "g5", "o1", "c6.9", "c2.9", "c3.9", "c7.9",
)


def mega_kernel(
    x_hbm, rank_hbm, kept_ref, g1_hbm, rw_hbm, wqkv_hbm, wout_hbm, g2_hbm, fc1, fc2, c_hbm,
    c_ref, x_ref, gw, g1w, g2w, small_out,
    rank_ref, g1_ref, rw_ref, g2_ref, wqkv, wout, w1, w2, xp, keep, gate, glogit, h1, h1t, qkv, probs, contextt, context, attended, middle,
    tok, cot, turned, out, gh2, out_part, gh2_part, out_sib, gh2_sib, out_near, gh2_near, out_far, gh2_far, hid, gpre, work,
    r1a, r1b, r2a, r2b, fz1, fz2, rz1, rz2,
    q0, q1, q2, q3, far, dg1, dg2, drw, sma, smr, smz,
    lsem, gsend, grecv, hsend, hrecv, csend, crecv, esend, erecv, s1s, s1r, s2s, s2r, s3s, s3r, fs, fr, ssib, rsib, free, chunk_free,
    qs, qr, small_sem, sms, smrs, smzs, smzr,
):
    patches, images, width = x_ref.shape
    t_own = xp.shape[0]
    tall = t_own // images
    half = width // 2
    part = w1.shape[1] // 2
    parts = (q0, q1, q2, q3)
    quarter = (width // 4, part // 4)
    r = lax.axis_index("rows")
    z = lax.axis_index("mlp")
    c, x, y = lax.rem(r, 2), lax.rem(lax.div(r, 2), 2), lax.rem(lax.div(r, 4), 2)
    r_sib, r_x, r_y = r + 1 - 2 * c, r + 2 - 4 * x, r + 4 - 8 * y
    r_diag = r_x + r_y - r
    z_pair, z_far = z + 1 - 2 * lax.rem(z, 2), z + 2 - 4 * lax.div(z, 2)
    q = 2 * y + x

    def ds(start, size):
        return pl.ds(pl.multiple_of(start, 16), size)

    def lanes(start, size):
        return pl.ds(pl.multiple_of(start, 128), size)

    def remote(src, dst, send, recv, row, column):
        return pltpu.make_async_remote_copy(
            src_ref=src, dst_ref=dst, send_sem=send, recv_sem=recv,
            device_id={"rows": row, "mlp": column}, device_id_type=MESH,
        )

    def release(semaphore, row):
        pl.semaphore_signal(semaphore, inc=1, device_id={"rows": row, "mlp": z}, device_id_type=MESH)

    def gather_copy(mat, kind):
        size = quarter[mat]
        sems = gsend.at[mat, kind], grecv.at[mat, kind]
        if mat == 0:
            place = w1.at[ds(q * size, size), pl.ds(part, part)]
            own = fc1.at[ds(q * size, size), lanes(c * part, part)]
        else:
            place = w2.at[ds(part + q * size, size), :]
            own = fc2.at[ds(c * part + q * size, size), :]
        if kind == 0:
            return remote(own, place, *sems, r, z_far)
        return remote(place, place, *sems, (r_x, r_y, r_diag)[kind - 1], z)

    def gather_forward(mat):
        gather_copy(mat, 0).wait_recv()
        for kind in (1, 2, 3):
            gather_copy(mat, kind).start()

    def own_shard(mat):
        if mat == 0:
            return pltpu.make_async_copy(fc1.at[:, lanes(c * part, part)], w1.at[:, pl.ds(0, part)], lsem.at[0])
        return pltpu.make_async_copy(fc2.at[ds(c * part, part), :], w2.at[pl.ds(0, part), :], lsem.at[1])

    load_qkv = pltpu.make_async_copy(wqkv_hbm, wqkv, lsem.at[2])
    load_out = pltpu.make_async_copy(wout_hbm, wout, lsem.at[3])
    load_x = pltpu.make_async_copy(x_hbm, x_ref, lsem.at[4])
    load_small = [
        pltpu.make_async_copy(src, dst, small_sem.at[k])
        for k, (src, dst) in enumerate(((rank_hbm, rank_ref), (g1_hbm, g1_ref), (rw_hbm, rw_ref), (g2_hbm, g2_ref)))
    ]
    load_c = pltpu.make_async_copy(c_hbm, c_ref, lsem.at[5])

    def token_copy(i, hop):
        start = (0, 0, 2 * t_own)[hop] + i * tall
        src, dst = tok.at[ds(start, tall), :], tok.at[ds((1, 2, 3)[hop] * t_own + i * tall, tall), :]
        row, column = (r, z_pair) if hop == 1 else (r_sib, z)
        return remote(src, dst, hsend.at[i, hop], hrecv.at[i, hop], row, column)

    def cot_copy(hop):
        src, dst = cot.at[ds((0, 0, 2)[hop] * t_own, t_own), :], cot.at[ds((1, 2, 3)[hop] * t_own, t_own), :]
        row, column = (r, z_pair) if hop == 1 else (r_sib, z)
        return remote(src, dst, csend.at[hop], crecv.at[hop], row, column)

    gh2_to_sib = remote(gh2_part.at[ds(0, t_own), :], gh2_sib, esend.at[0], erecv.at[0], r_sib, z)
    out_to_sib = remote(out_part.at[ds(0, t_own), :], out_sib, esend.at[1], erecv.at[1], r_sib, z)
    out_over = remote(out_part.at[ds(2 * t_own, t_own), :], out_near, esend.at[2], erecv.at[2], r_sib, z)
    out_far_copy = remote(out_part.at[ds(t_own, t_own), :], out_far, esend.at[3], erecv.at[3], r, z_pair)

    def gh2_over(i):
        src = gh2_part.at[ds(2 * t_own + i * tall, tall), :]
        return remote(src, gh2_near.at[ds(i * tall, tall), :], esend.at[4 + i], erecv.at[4 + i], r_sib, z)

    def gh2_far_copy(i):
        src = gh2_part.at[ds(t_own + i * tall, tall), :]
        return remote(src, gh2_far.at[ds(i * tall, tall), :], esend.at[6 + i], erecv.at[6 + i], r, z_pair)

    fc_whole, fc_half, fc_quarter, fc_done, fc_far = (g1w, g2w), (r1a, r1b), (r2a, r2b), (fz1, fz2), (rz1, rz2)
    fc_rows = ((width // 2, width // 4), (part // 2, part // 4))

    def fc_ways(k, m):
        shard = lax.div(z, 2) if k == 0 else 1 - lax.div(z, 2)
        turn = lax.rem(shard + m, 2)
        return r_x + (r_y - r_x) * turn, r_y + (r_x - r_y) * turn, x + (y - x) * turn, y + (x - y) * turn

    def fc_first(k, m):
        n1, _, a1, _ = fc_ways(k, m)
        rows, _ = fc_rows[m]
        src = fc_whole[m].at[k, ds((1 - a1) * rows, rows), :]
        return remote(src, fc_half[m].at[k], s1s.at[k, m], s1r.at[k, m], n1, z)

    def fc_second(k, m):
        _, n2, a1, a2 = fc_ways(k, m)
        rows, less = fc_rows[m]
        src = fc_whole[m].at[k, ds(a1 * rows + (1 - a2) * less, less), :]
        return remote(src, fc_quarter[m].at[k], s2s.at[k, m], s2r.at[k, m], n2, z)

    fc_third = [remote(fc_done[m].at[1], fc_far[m], s3s.at[m], s3r.at[m], r, z_far) for m in range(2)]

    def fc_spread(level, m):
        n1, n2, a1, a2 = fc_ways(0, m)
        rows, less = fc_rows[m]
        place = ds(a1 * rows + a2 * less, less) if level == 0 else ds(a1 * rows, rows)
        held = fc_whole[m].at[0, place, :]
        return remote(held, held, fs.at[level, m], fr.at[level, m], n2 if level == 0 else n1, z)

    fc_share = (
        remote(g1w.at[0], g1w.at[1], ssib.at[0], rsib.at[0], r_sib, z),
        remote(g2w.at[0], g2w.at[1], ssib.at[1], rsib.at[1], r_sib, z),
    )

    def fc_fold_second(k, m):
        fc_first(k, m).wait_recv()
        _, _, a1, a2 = fc_ways(k, m)
        rows, less = fc_rows[m]
        place, whole = ds(a1 * rows + (1 - a2) * less, less), fc_whole[m]
        whole[k, place, :] = whole[k, place, :] + fc_half[m][k, ds((1 - a2) * less, less), :]
        fc_second(k, m).start()

    def fc_fold_third(k):
        for m in range(2):
            fc_second(k, m).wait_recv()
            _, _, a1, a2 = fc_ways(k, m)
            rows, less = fc_rows[m]
            total = fc_whole[m][k, ds(a1 * rows + a2 * less, less), :].astype(F32)
            total = total + fc_half[m][k, ds(a2 * less, less), :].astype(F32) + fc_quarter[m][k].astype(F32)
            fc_done[m][k] = total.astype(BF)
        if k == 1:
            for copy in fc_third:
                copy.start()
        for m in range(2):
            fc_first(k, m).wait_send()
            fc_second(k, m).wait_send()
        if k == 1:
            release(free.at[0], r_sib)
        else:
            release(free.at[1], r_x)
            release(free.at[1], r_y)

    def fc_finish():
        for copy in fc_third:
            copy.wait_recv()
        pl.semaphore_wait(free.at[1], 2)
        for m in range(2):
            _, _, a1, a2 = fc_ways(0, m)
            rows, less = fc_rows[m]
            fc_whole[m][0, ds(a1 * rows + a2 * less, less), :] = fc_done[m][0] + fc_far[m][...]
            fc_spread(0, m).start()

    def fc_widen():
        for m in range(2):
            fc_spread(0, m).wait_recv()
        for m in range(2):
            fc_spread(1, m).start()

    def fc_to_sibling():
        for m in range(2):
            fc_spread(1, m).wait_recv()
        pl.semaphore_wait(free.at[0], 1)
        for copy in fc_share:
            copy.start()

    sizes = tuple(width >> level for level in range(1, 5))

    def hops(j):
        ways = {"x": (r_x, z, x), "y": (r_y, z, y), "z": (r, z_pair, lax.rem(z, 2))}
        return [(r_sib, z, c)] + [ways[axis] for axis in PATHS[j]]

    def base(path, level):
        start = 0
        for (_, _, bit), size in zip(path[:level], sizes):
            start = start + bit * size
        return start

    def core_copy(j):
        src = gw.at[j, :, ds((1 - c) * half, half), :]
        return remote(src, parts[0].at[j], qs.at[j, 0], qr.at[j, 0], r_sib, z)

    def chunk_copy(j, step):
        path = hops(j)
        if step == 0:
            return core_copy(j)
        if step < 4:
            row, column, bit = path[step]
            start = base(path, step) + (1 - bit) * sizes[step]
            return remote(gw.at[j, :, ds(start, sizes[step]), :], parts[step].at[j], qs.at[j, step], qr.at[j, step], row, column)
        if step == 4:
            own = gw.at[j, :, ds(base(path, 4), sizes[3]), :]
            return remote(own, far.at[j], qs.at[j, 4], qr.at[j, 4], r, z_far)
        level = 8 - step
        row, column, _ = path[level]
        held = gw.at[j, :, ds(base(path, level + 1), sizes[level]), :]
        return remote(held, held, qs.at[j, step], qr.at[j, step], row, column)

    def chunk_step(j, step):
        path = hops(j)
        chunk_copy(j, step - 1).wait()
        if step <= 4:
            row, column, _ = path[step - 1]
            pl.semaphore_signal(
                chunk_free.at[j, step - 1], inc=1, device_id={"rows": row, "mlp": column}, device_id_type=MESH
            )
            start = base(path, min(step, 4))
            if step < 4:
                start = base(path, step) + (1 - path[step][2]) * sizes[step]
            size = sizes[min(step, 3)]
            total = gw[j, :, ds(start, size), :].astype(F32)
            for level in range(step):
                total = total + parts[level][j, :, ds(start - base(path, level + 1), size), :].astype(F32)
            gw[j, :, ds(start, size), :] = total.astype(BF)
        if step == 5:
            own = ds(base(path, 4), sizes[3])
            gw[j, :, own, :] = gw[j, :, own, :] + far[j]
        if 5 <= step <= 8:
            pl.semaphore_wait(chunk_free.at[j, 8 - step], 1)
        if step <= 8:
            chunk_copy(j, step).start()

    def small_copy(level):
        row = (r_sib, r_x, r_y)[level]
        return remote(sma.at[level], smr.at[level], sms.at[level], smrs.at[level], row, z)

    def small_z(step):
        src, dst = smz.at[2 * step], smz.at[2 * step + 1]
        return remote(src, dst, smzs.at[step], smzr.at[step], r, (z_pair, z_far)[step])

    barrier = pltpu.get_barrier_semaphore()
    partners = ((r_sib, z), (r_x, z), (r_y, z), (r_diag, z), (r, z_pair), (r, z_far))
    for row, column in partners:
        pl.semaphore_signal(barrier, inc=1, device_id={"rows": row, "mlp": column}, device_id_type=MESH)
    load_c.start()
    load_x.start()
    for copy in load_small:
        copy.start()
    load_qkv.start()
    load_out.start()
    own_shard(0).start()
    own_shard(1).start()
    pl.semaphore_wait(barrier, len(partners))
    gather_copy(0, 0).start()
    gather_copy(1, 0).start()
    load_c.wait()
    for i in range(images):
        work[...] = jnp.zeros_like(work)
        work[0:patches, :] = c_ref[:, i, :]
        cot[i * tall : (i + 1) * tall, :] = work[...]
    cot_copy(0).start()
    cot_copy(1).start()
    load_x.wait()
    for copy in load_small:
        copy.wait()
    for i in range(images):
        forward_rows(i, x_ref, rank_ref, kept_ref, g1_ref, rw_ref, xp, keep, gate, h1, work)

    load_qkv.wait()

    @pl.loop(0, 3 * width // 256)
    def _(j):
        forward_qkv(j, h1, wqkv, qkv)

    @pl.loop(0, HEADS // 2)
    def _(p):
        for i in range(images):
            attend(p, i, width, tall, qkv, keep, probs, context, contextt)

        @pl.when(p == 2)
        def _():
            gather_forward(0)

        @pl.when(p == 5)
        def _():
            gather_forward(1)

    load_out.wait()

    @pl.loop(0, images)
    def _(i):
        forward_out(i, tall, context, wout, xp, keep, gate, g2_ref, attended, middle, tok)
        token_copy(i, 0).start()
        token_copy(i, 1).start()

    own_shard(0).wait()
    own_shard(1).wait()

    def at(block, number, do):
        @pl.when(block == number)
        def _():
            do()

    def before_sibling():
        for i in range(images):
            token_copy(i, 0).wait_recv()
        cot_copy(0).wait_recv()

    h1t[...] = h1[...].T

    @pl.loop(0, 2 * images)
    def _(block):
        at(block, images, before_sibling)
        rows = ds(block * tall, tall)
        hid[rows, 0:part], gpre[rows, 0:part] = mlp_rows(tok[rows, :], cot[rows, :], w1[:, 0:part], w2[0:part, :])

    cot_copy(1).wait_recv()
    cot_copy(2).start()
    for mat in range(2):
        for kind in (1, 2, 3):
            gather_copy(mat, kind).wait_recv()
    for ref in (dg1, dg2, drw):
        ref[...] = jnp.zeros_like(ref)

    def before_near():
        cot_copy(2).wait_recv()
        gh2_to_sib.start()
        out_to_sib.start()

    def forward_token(i):
        token_copy(i, 1).wait_recv()
        token_copy(i, 2).start()

    def send_far(i):
        gh2_over(i).wait_recv()
        rows = ds(t_own + i * tall, tall)
        gh2_part[rows, :] = gh2_part[rows, :] + gh2_near[ds(i * tall, tall), :]
        gh2_far_copy(i).start()

    def before_last():
        send_far(0)
        token_copy(1, 2).wait_recv()

    @pl.loop(0, 8)
    def _(block):
        at(block, 3, lambda: forward_token(0))
        at(block, 4, before_near)
        at(block, 5, lambda: token_copy(0, 2).wait_recv())
        at(block, 6, lambda: forward_token(1))
        at(block, 7, before_last)
        inner = lax.rem(block, 5)
        swap = lax.div(block, 5) * (1 - 2 * inner + 3 * lax.div(inner * (inner - 1), 2))
        spot = block + swap
        rows = ds(spot * tall, tall)

        @pl.when(block < 2 * images)
        def _():
            hid[rows, part:], gpre[rows, part:] = mlp_rows(tok[rows, :], cot[rows, :], w1[:, part:], w2[part:, :])

        @pl.when(block >= 2 * images)
        def _():
            hid[rows, :], gpre[rows, :] = mlp_rows(tok[rows, :], cot[rows, :], w1[...], w2[...])

        share_out = dot_nn(hid[rows, :], w2[...])
        share_gh2 = dot_nt(gpre[rows, :], w1[...])

        @pl.when(block < images)
        def _():
            out[rows, :] = share_out
            gh2[rows, :] = share_gh2

        @pl.when(block >= images)
        def _():
            there = ds(lax.max(spot - images, 0) * tall, tall)
            out_part[there, :] = share_out.astype(BF)
            gh2_part[there, :] = share_gh2.astype(BF)

        at(block, 5, lambda: gh2_over(0).start())
        at(block, 7, lambda: gh2_over(1).start())

    out_over.start()
    turned[...] = tok[...].T
    for m in range(3):
        rows = slice(m * width // 3, (m + 1) * width // 3)
        total = dot_nn(turned[rows, :], gpre[...]).astype(BF)
        g1w[0, rows, :] = total[:, 0:part]
        g1w[1, rows, :] = total[:, part:]
    for k in range(2):
        fc_first(k, 0).start()
    send_far(1)
    turned[...] = hid[...].T
    for m in range(2):
        g2w[m] = dot_nn(turned[m * part : (m + 1) * part, :], cot[...]).astype(BF)
    for k in range(2):
        fc_first(k, 1).start()

    def back_image(i):
        if i == 0:
            gh2_to_sib.wait_recv()
            for n in range(images):
                token_copy(n, 0).wait_send()
                token_copy(n, 1).wait_send()
        gh2_far_copy(i).wait_recv()
        rows = pl.ds(i * tall, tall)
        gh2[rows, :] += gh2_sib[rows, :].astype(F32) + gh2_far[rows, :].astype(F32)
        back_rows(i, tall, cot, gh2, middle, keep, gate, attended, g2_ref, gh2, tok, glogit, dg2)
        context[rows, :] = dot_nt(tok[rows, :], wout[...]).astype(BF)

    def fill(j, total):
        for b in range(3):
            gw[j, b] = total[:, b * 128 : (b + 1) * 128].astype(BF)
        core_copy(j).start()

    def grad_out_half(n):
        total = 0.0
        for i in range(images):
            total = total + dot_nn(contextt[i], tok[i * tall : (i + 1) * tall, n * half : (n + 1) * half])
        fill(n, total)

    def pair_chunk(p):
        fill(p + 2, dot_nn(h1t[...], pair_columns(qkv, p, width)))

    def finish(i):
        rows = pl.ds(i * tall, tall)
        dy = dot_nt(qkv[rows, :], wqkv[...])
        back_input(i, tall, dy, glogit, rw_ref, xp, h1, g1_ref, gh2, x_ref, dg1, drw)
        if i == images - 1:
            sma[0] = jnp.concatenate([dg1[...], drw[...], dg2[...], jnp.zeros((5, width), F32)], 0)
            small_copy(0).start()

    def small_step(step):
        if step < 3:
            small_copy(step - 1).wait()
            sma[step] = sma[step - 1] + smr[step - 1]
            small_copy(step).start()
        elif step == 3:
            small_copy(2).wait()
            smz[0] = sma[2] + smr[2]
            small_z(0).start()
        else:
            small_z(step - 4).wait()
            if step == 4:
                smz[2] = smz[0] + smz[1]
                small_z(1).start()
            else:
                small_out[...] = smz[2] + smz[3]

    def out_send():
        out_over.wait_recv()
        rows = pl.ds(t_own, t_own)
        out_part[rows, :] = out_part[rows, :] + out_near[...]
        out_far_copy.start()

    def out_finish(i):
        if i == 0:
            out_to_sib.wait_recv()
            out_far_copy.wait_recv()
        rows = pl.ds(i * tall, tall)
        total = middle[rows, :] + out[rows, :] + out_sib[rows, :].astype(F32) + out_far[rows, :].astype(F32)
        c_ref[:, i, :] = total.astype(BF)[0:patches, :]

    def fc_share_end():
        for copy in fc_share:
            copy.wait()

    single = {"fc": fc_finish, "fd": fc_widen, "fe": fc_to_sibling, "ff": fc_share_end, "osend": out_send}
    numbered = (("finish", finish), ("back", back_image), ("out", grad_out_half),
                ("fb", fc_fold_third), ("g", small_step), ("o", out_finish))

    def perform(names):
        for name in names:
            if name in single:
                single[name]()
            elif name[:2] == "fa":
                fc_fold_second(int(name[2]), int(name[3]))
            elif name[0] == "c":
                chunk_step(int(name[1]), int(name[3]))
            else:
                do = next(f for head, f in numbered if name[:-1] == head)
                do(int(name[-1]))

    first, start, stop = ORDER.index("pairs0"), ORDER.index("pairs1"), ORDER.index("last2")
    perform(ORDER[:first])

    @pl.loop(0, HEADS // 4)
    def _(n):
        for p in (2 * n, 2 * n + 1):
            attend_back(p, 0, width, tall, qkv, probs, context)

    perform(ORDER[first + 1 : start])
    marks = [ORDER.index(name) for k in range(3) for name in ("pairs%d" % (k + 1), "last%d" % k)]

    @pl.loop(0, HEADS // 4)
    def _(n):
        for p in (2 * n, 2 * n + 1):
            attend_back(p, 1, width, tall, qkv, probs, context)
        pair_chunk(2 * n)
        for k in range(3):
            at(n, k, lambda k=k: perform(ORDER[marks[2 * k] + 1 : marks[2 * k + 1]]))
        pair_chunk(2 * n + 1)
        for k in range(2):
            at(n, k, lambda k=k: perform(ORDER[marks[2 * k + 1] + 1 : marks[2 * k + 2]]))

    perform(ORDER[stop + 1 :])
    for level in range(2):
        for m in range(2):
            fc_spread(level, m).wait_send()
    for copy in fc_third:
        copy.wait_send()
    for mat in range(2):
        for kind in range(4):
            gather_copy(mat, kind).wait_send()
    for i in range(images):
        token_copy(i, 2).wait_send()
        gh2_over(i).wait_send()
        gh2_far_copy(i).wait_send()
    for hop in range(3):
        cot_copy(hop).wait_send()
    for copy in (gh2_to_sib, out_to_sib, out_over, out_far_copy):
        copy.wait_send()


VMEM = pl.BlockSpec(memory_space=pltpu.VMEM)
SMEM = pl.BlockSpec(memory_space=pltpu.SMEM)
ANY = pl.BlockSpec(memory_space=pl.ANY)


def widen_kernel(
    block, gx, gw, gf1, gf2, small, block_out, gx_out, gq_out, go_out, f1_out, f2_out, g1_out, rw_out, g2_out,
    gq_wide, go_wide, f1_wide, f2_wide, store_sem, pass_sem,
):
    _, width, part = gf1.shape
    step = width // WIDEN
    c = lax.rem(lax.axis_index("rows"), 2)
    passed = [pltpu.make_async_copy(src, dst, pass_sem.at[k]) for k, (src, dst) in enumerate(((block, block_out), (gx, gx_out)))]

    def rows_of(i):
        return pl.ds(pl.multiple_of(i * step, 16), step)

    def stores(i):
        rows = rows_of(i)
        pairs = ((gq_wide, gq_out), (go_wide, go_out), (f1_wide, f1_out), (f2_wide, f2_out))
        return [
            pltpu.make_async_copy(src.at[rows, :], dst.at[rows, :], store_sem.at[i, k]) for k, (src, dst) in enumerate(pairs)
        ]

    @pl.loop(0, WIDEN)
    def _(i):
        rows = rows_of(i)
        for p in range(CHUNKS - 2):
            for b in range(3):
                start = b * width + p * 128
                gq_wide[rows, start : start + 128] = gw[2 + p, b, rows, :].astype(F32)
        for b in range(6):
            go_wide[rows, b * 128 : (b + 1) * 128] = gw[b // 3, b % 3, rows, :].astype(F32)
        for k in range(2):
            core = c + k - 2 * c * k
            f1_wide[rows, pl.ds(pl.multiple_of(core * part, 128), part)] = gf1[k, rows, :].astype(F32)
        core = lax.div(i * step, part)
        inner = pl.ds(pl.multiple_of(i * step - core * part, 16), step)
        f2_wide[rows, :] = gf2[core + c - 2 * core * c, inner, :].astype(F32)
        for copy in stores(i):
            copy.start()

    for copy in passed:
        copy.start()
    g1_out[...], rw_out[...], g2_out[...] = small[0], small[1], small[2]

    @pl.loop(0, WIDEN)
    def _(i):
        for copy in stores(i):
            copy.wait()

    for copy in passed:
        copy.wait()


def widen(*held):
    width = held[3].shape[1]
    tokens = jax.ShapeDtypeStruct(held[0].shape, BF)
    wide = [(width, 3 * width), (width, width), (width, width), (width, width)]
    return pl.pallas_call(
        widen_kernel,
        out_shape=[tokens, tokens] + [jax.ShapeDtypeStruct(dims, F32) for dims in wide] + [jax.ShapeDtypeStruct((width,), F32)] * 3,
        in_specs=[VMEM] * 6,
        out_specs=[ANY] * 6 + [VMEM] * 3,
        scratch_shapes=[pltpu.VMEM(dims, F32) for dims in wide]
        + [pltpu.SemaphoreType.DMA((WIDEN, 4)), pltpu.SemaphoreType.DMA((2,))],
        compiler_params=pltpu.CompilerParams(vmem_limit_bytes=32 * 1024 * 1024),
        name="widen",
    )(*(pltpu.with_memory_space_constraint(a, pltpu.VMEM) for a in held))


def per_device(others, images, patch_rank, kept_count, ln1_gain, router_weight, w_qkv, w_out, ln2_gain, w_fc1, w_fc2, cotangent):
    count, patches, width = images.shape
    tall = -(-patches // 16) * 16
    t = count * tall
    part = w_fc1.shape[1] // 2
    half, eighth = width // 2, width // 8

    def bf(*dims):
        return pltpu.VMEM(dims, BF)

    def f32(*dims):
        return pltpu.VMEM(dims, F32)

    def sem(*dims):
        return pltpu.SemaphoreType.DMA(dims)

    scratch = [
        pltpu.VMEM(patch_rank.shape, jnp.int32), f32(width), bf(width), f32(width),
        bf(width, 3 * width), bf(width, width), bf(width, 2 * part), bf(2 * part, width),
        bf(t, width), f32(t, 128), f32(t, 128), f32(t, 128), bf(t, width), bf(width, t), bf(t, 3 * width),
        f32(count, HEADS, tall, tall), bf(count, width, tall), bf(t, width), f32(t, width), f32(t, width),
        bf(4 * t, width), bf(4 * t, width), bf(width, 4 * t), f32(t, width), f32(t, width),
        bf(3 * t, width), bf(3 * t, width), bf(t, width), bf(t, width), bf(t, width), bf(t, width), bf(t, width), bf(t, width),
        bf(4 * t, 2 * part), bf(4 * t, 2 * part), bf(tall, width),
        bf(2, width // 2, part), bf(2, part // 2, width), bf(2, width // 4, part), bf(2, part // 4, width),
        bf(2, width // 4, part), bf(2, part // 4, width), bf(width // 4, part), bf(part // 4, width),
        bf(CHUNKS, 3, half, 128), bf(CHUNKS, 3, 2 * eighth, 128), bf(CHUNKS, 3, eighth, 128),
        bf(CHUNKS, 3, eighth // 2, 128), bf(CHUNKS, 3, eighth // 2, 128),
        f32(1, width), f32(1, width), f32(1, width), f32(3, 8, width), f32(3, 8, width), f32(4, 8, width),
        sem(6), sem(2, 4), sem(2, 4), sem(count, 3), sem(count, 3), sem(3), sem(3), sem(8), sem(8),
        sem(2, 2), sem(2, 2), sem(2, 2), sem(2, 2), sem(2), sem(2),
        sem(2, 2), sem(2, 2), sem(2), sem(2), pltpu.SemaphoreType.REGULAR((2,)), pltpu.SemaphoreType.REGULAR((CHUNKS, 4)),
        sem(CHUNKS, 9), sem(CHUNKS, 9), sem(4),
        sem(3), sem(3), sem(2), sem(2),
    ]

    block, gx, gw, gf1, gf2, small = pl.pallas_call(
        mega_kernel,
        out_shape=[
            bf(patches, count, width), bf(patches, count, width), bf(CHUNKS, 3, width, 128),
            bf(2, width, part), bf(2, part, width), f32(8, width),
        ],
        in_specs=[ANY, ANY, SMEM] + [ANY] * 8,
        out_specs=[VMEM] * 6,
        scratch_shapes=scratch,
        compiler_params=pltpu.CompilerParams(
            collective_id=0, has_side_effects=True, vmem_limit_bytes=int(55.5 * 1024) * 1024
        ),
        name="block",
    )(images.transpose(1, 0, 2), patch_rank, kept_count, ln1_gain, router_weight, w_qkv, w_out, ln2_gain, w_fc1, w_fc2,
      cotangent.transpose(1, 0, 2))
    block, gx, gq, go, f1, f2, g1, rw, g2 = widen(block, gx, gw, gf1, gf2, small)
    if others:
        gq, go, f1, f2, g1, rw, g2 = lax.psum((gq, go, f1, f2, g1, rw, g2), "rows", axis_index_groups=others)
    return block.transpose(1, 0, 2), gx.transpose(1, 0, 2), g1, rw, gq, go, g2, f1, f2


def solution(mesh):
    rows = mesh.shape["rows"]
    others = [[8 * g + i for g in range(rows // 8)] for i in range(8)] if rows > 8 else None
    return jax.shard_map(
        functools.partial(per_device, others),
        mesh=mesh,
        in_specs=(
            P(("rows", "mlp"), None, None), P(("rows", "mlp"), None), P(("rows", "mlp")), P(), P(), P(), P(), P(),
            P(None, "mlp"), P("mlp", None), P(("rows", "mlp"), None, None),
        ),
        out_specs=(
            P(("rows", "mlp"), None, None), P(("rows", "mlp"), None, None), P(), P(), P(), P(), P(),
            P(None, "mlp"), P("mlp", None),
        ),
        check_vma=False,
    )
```

profile of v0, /device:TPU:0, one launch (start us, length us, event | category | flops | bytes accessed | tf_op | source)
XLA Modules:
  0.0 127.5 jit_solution(7684616788841644656)
XLA Ops:
  0.6 120.3 %block.1 = (bf16[197,2,768]{2,1,0:T(2,128)(2,1)S(1)}, bf16[197,2,768]{2,1,0:T(2,128)(2,1)S(1)}, bf16[8,3,768,128]{3,2,1,0:T(8,128)(2,1)S(1)}, bf16[2,768,384]{2,...) custom-call(bf16[197,2,768]{2,1,0:T(2,128)(2,1)} %bitcast.4, s32[2,197]{1,0:T(2,128)} %rank_hbm.1, ...), custom_call_target="tpu_custom_call" | custom-call | tf_op jit(solution)/shard_map/block/pallas_call | solution.py:820
  121.0 6.3 %widen.1 = (bf16[197,2,768]{2,1,0:T(2,128)(2,1)}, bf16[197,2,768]{2,1,0:T(2,128)(2,1)}, f32[768,2304]{1,0:T(8,128)}, f32[768,768]{1,0:T(8,128)}, f32[768,768]{1,...) custom-call(bf16[197,2,768]{2,1,0:T(2,128)(2,1)S(1)} %get-tuple-element.24.block, ...), custom_call_target="tpu_custom_call" | custom-call | tf_op jit(solution)/shard_map/widen/pallas_call | solution.py:772
where the time goes:
time: 128 us; the launch traced here: 127 us
  Pallas kernels  127 us (99%)
    pallas_call x1, Pallas kernels, per_device(): pl.pallas_call(mega_kernel, out_shape=[bf(patches, count, width), bf(patc...  120 us
    pallas_call x1, Pallas kernels, widen(): pl.pallas_call(widen_kernel, out_shape=[tokens, tokens] + [jax.ShapeDtype...  6.33 us

commit v1 on v0

--- a/solution.py
+++ b/solution.py
@@ -184,9 +184,9 @@
 
 
 def mega_kernel(
-    x_hbm, rank_hbm, kept_ref, g1_hbm, rw_hbm, wqkv_hbm, wout_hbm, g2_hbm, fc1, fc2, c_hbm,
+    x_hbm, rank_hbm, kept_hbm, g1_hbm, rw_hbm, wqkv_hbm, wout_hbm, g2_hbm, fc1, fc2, c_hbm,
     c_ref, x_ref, gw, g1w, g2w, small_out,
-    rank_ref, g1_ref, rw_ref, g2_ref, wqkv, wout, w1, w2, xp, keep, gate, glogit, h1, h1t, qkv, probs, contextt, context, attended, middle,
+    rank_ref, kept_ref, g1_ref, rw_ref, g2_ref, wqkv, wout, w1, w2, xp, keep, gate, glogit, h1, h1t, qkv, probs, contextt, context, attended, middle,
     tok, cot, turned, out, gh2, out_part, gh2_part, out_sib, gh2_sib, out_near, gh2_near, out_far, gh2_far, hid, gpre, work,
     r1a, r1b, r2a, r2b, fz1, fz2, rz1, rz2,
     q0, q1, q2, q3, far, dg1, dg2, drw, sma, smr, smz,
@@ -251,7 +251,7 @@
     load_x = pltpu.make_async_copy(x_hbm, x_ref, lsem.at[4])
     load_small = [
         pltpu.make_async_copy(src, dst, small_sem.at[k])
-        for k, (src, dst) in enumerate(((rank_hbm, rank_ref), (g1_hbm, g1_ref), (rw_hbm, rw_ref), (g2_hbm, g2_ref)))
+        for k, (src, dst) in enumerate(((rank_hbm, rank_ref), (kept_hbm, kept_ref), (g1_hbm, g1_ref), (rw_hbm, rw_ref), (g2_hbm, g2_ref)))
     ]
     load_c = pltpu.make_async_copy(c_hbm, c_ref, lsem.at[5])
 
@@ -377,7 +377,7 @@
         return start
 
     def core_copy(j):
-        src = gw.at[j, :, ds((1 - c) * half, half), :]
+        src = gw.at[j, ds((1 - c) * half, half), :]
         return remote(src, parts[0].at[j], qs.at[j, 0], qr.at[j, 0], r_sib, z)
 
     def chunk_copy(j, step):
@@ -387,13 +387,13 @@
         if step < 4:
             row, column, bit = path[step]
             start = base(path, step) + (1 - bit) * sizes[step]
-            return remote(gw.at[j, :, ds(start, sizes[step]), :], parts[step].at[j], qs.at[j, step], qr.at[j, step], row, column)
+            return remote(gw.at[j, ds(start, sizes[step]), :], parts[step].at[j], qs.at[j, step], qr.at[j, step], row, column)
         if step == 4:
-            own = gw.at[j, :, ds(base(path, 4), sizes[3]), :]
+            own = gw.at[j, ds(base(path, 4), sizes[3]), :]
             return remote(own, far.at[j], qs.at[j, 4], qr.at[j, 4], r, z_far)
         level = 8 - step
         row, column, _ = path[level]
-        held = gw.at[j, :, ds(base(path, level + 1), sizes[level]), :]
+        held = gw.at[j, ds(base(path, level + 1), sizes[level]), :]
         return remote(held, held, qs.at[j, step], qr.at[j, step], row, column)
 
     def chunk_step(j, step):
@@ -408,13 +408,13 @@
             if step < 4:
                 start = base(path, step) + (1 - path[step][2]) * sizes[step]
             size = sizes[min(step, 3)]
-            total = gw[j, :, ds(start, size), :].astype(F32)
+            total = gw[j, ds(start, size), :].astype(F32)
             for level in range(step):
-                total = total + parts[level][j, :, ds(start - base(path, level + 1), size), :].astype(F32)
-            gw[j, :, ds(start, size), :] = total.astype(BF)
+                total = total + parts[level][j, ds(start - base(path, level + 1), size), :].astype(F32)
+            gw[j, ds(start, size), :] = total.astype(BF)
         if step == 5:
             own = ds(base(path, 4), sizes[3])
-            gw[j, :, own, :] = gw[j, :, own, :] + far[j]
+            gw[j, own, :] = gw[j, own, :] + far[j]
         if 5 <= step <= 8:
             pl.semaphore_wait(chunk_free.at[j, 8 - step], 1)
         if step <= 8:
@@ -597,8 +597,7 @@
         context[rows, :] = dot_nt(tok[rows, :], wout[...]).astype(BF)
 
     def fill(j, total):
-        for b in range(3):
-            gw[j, b] = total[:, b * 128 : (b + 1) * 128].astype(BF)
+        gw[j] = total.astype(BF)
         core_copy(j).start()
 
     def grad_out_half(n):
@@ -711,7 +710,6 @@
 
 
 VMEM = pl.BlockSpec(memory_space=pltpu.VMEM)
-SMEM = pl.BlockSpec(memory_space=pltpu.SMEM)
 ANY = pl.BlockSpec(memory_space=pl.ANY)
 
 
@@ -740,9 +738,9 @@
         for p in range(CHUNKS - 2):
             for b in range(3):
                 start = b * width + p * 128
-                gq_wide[rows, start : start + 128] = gw[2 + p, b, rows, :].astype(F32)
-        for b in range(6):
-            go_wide[rows, b * 128 : (b + 1) * 128] = gw[b // 3, b % 3, rows, :].astype(F32)
+                gq_wide[rows, start : start + 128] = gw[2 + p, rows, b * 128 : (b + 1) * 128].astype(F32)
+        for h in range(2):
+            go_wide[rows, h * part : (h + 1) * part] = gw[h, rows, :].astype(F32)
         for k in range(2):
             core = c + k - 2 * c * k
             f1_wide[rows, pl.ds(pl.multiple_of(core * part, 128), part)] = gf1[k, rows, :].astype(F32)
@@ -798,7 +796,7 @@
         return pltpu.SemaphoreType.DMA(dims)
 
     scratch = [
-        pltpu.VMEM(patch_rank.shape, jnp.int32), f32(width), bf(width), f32(width),
+        pltpu.VMEM(patch_rank.shape, jnp.int32), pltpu.SMEM(kept_count.shape, jnp.int32), f32(width), bf(width), f32(width),
         bf(width, 3 * width), bf(width, width), bf(width, 2 * part), bf(2 * part, width),
         bf(t, width), f32(t, 128), f32(t, 128), f32(t, 128), bf(t, width), bf(width, t), bf(t, 3 * width),
         f32(count, HEADS, tall, tall), bf(count, width, tall), bf(t, width), f32(t, width), f32(t, width),
@@ -807,23 +805,23 @@
         bf(4 * t, 2 * part), bf(4 * t, 2 * part), bf(tall, width),
         bf(2, width // 2, part), bf(2, part // 2, width), bf(2, width // 4, part), bf(2, part // 4, width),
         bf(2, width // 4, part), bf(2, part // 4, width), bf(width // 4, part), bf(part // 4, width),
-        bf(CHUNKS, 3, half, 128), bf(CHUNKS, 3, 2 * eighth, 128), bf(CHUNKS, 3, eighth, 128),
-        bf(CHUNKS, 3, eighth // 2, 128), bf(CHUNKS, 3, eighth // 2, 128),
+        bf(CHUNKS, half, 384), bf(CHUNKS, 2 * eighth, 384), bf(CHUNKS, eighth, 384),
+        bf(CHUNKS, eighth // 2, 384), bf(CHUNKS, eighth // 2, 384),
         f32(1, width), f32(1, width), f32(1, width), f32(3, 8, width), f32(3, 8, width), f32(4, 8, width),
         sem(6), sem(2, 4), sem(2, 4), sem(count, 3), sem(count, 3), sem(3), sem(3), sem(8), sem(8),
         sem(2, 2), sem(2, 2), sem(2, 2), sem(2, 2), sem(2), sem(2),
         sem(2, 2), sem(2, 2), sem(2), sem(2), pltpu.SemaphoreType.REGULAR((2,)), pltpu.SemaphoreType.REGULAR((CHUNKS, 4)),
-        sem(CHUNKS, 9), sem(CHUNKS, 9), sem(4),
+        sem(CHUNKS, 9), sem(CHUNKS, 9), sem(5),
         sem(3), sem(3), sem(2), sem(2),
     ]
 
     block, gx, gw, gf1, gf2, small = pl.pallas_call(
         mega_kernel,
         out_shape=[
-            bf(patches, count, width), bf(patches, count, width), bf(CHUNKS, 3, width, 128),
+            bf(patches, count, width), bf(patches, count, width), bf(CHUNKS, width, 384),
             bf(2, width, part), bf(2, part, width), f32(8, width),
         ],
-        in_specs=[ANY, ANY, SMEM] + [ANY] * 8,
+        in_specs=[ANY] * 11,
         out_specs=[VMEM] * 6,
         scratch_shapes=scratch,
         compiler_params=pltpu.CompilerParams(

time: 128 us -> 127 us (level)
  no operation moved by 1% of the time
where the time goes in v1:
time: 127 us
  Pallas kernels  126 us (99%)
    pallas_call x1, Pallas kernels, per_device(): pl.pallas_call(mega_kernel, out_shape=[bf(patches, count, width), bf(patc...  120 us
    pallas_call x1, Pallas kernels, widen(): pl.pallas_call(widen_kernel, out_shape=[tokens, tokens] + [jax.ShapeDtype...  6.33 us

profile of v1, /device:TPU:0, one launch (start us, length us, event | category | flops | bytes accessed | tf_op | source)
XLA Modules:
  0.0 127.0 jit_solution(16013375584257167818)
XLA Ops:
  0.6 119.8 %block.1 = (bf16[197,2,768]{2,1,0:T(2,128)(2,1)S(1)}, bf16[197,2,768]{2,1,0:T(2,128)(2,1)S(1)}, bf16[8,768,384]{2,1,0:T(8,128)(2,1)S(1)}, bf16[2,768,384]{2,1,0:...) custom-call(bf16[197,2,768]{2,1,0:T(2,128)(2,1)} %bitcast.4, s32[2,197]{1,0:T(2,128)} %rank_hbm.1, ...), custom_call_target="tpu_custom_call" | custom-call | tf_op jit(solution)/shard_map/block/pallas_call | solution.py:818
  120.5 6.3 %widen.1 = (bf16[197,2,768]{2,1,0:T(2,128)(2,1)}, bf16[197,2,768]{2,1,0:T(2,128)(2,1)}, f32[768,2304]{1,0:T(8,128)}, f32[768,768]{1,0:T(8,128)}, f32[768,768]{1,...) custom-call(bf16[197,2,768]{2,1,0:T(2,128)(2,1)S(1)} %get-tuple-element.24.block, ...), custom_call_target="tpu_custom_call" | custom-call | tf_op jit(solution)/shard_map/widen/pallas_call | solution.py:770

commit v2 on v1

--- a/solution.py
+++ b/solution.py
@@ -170,16 +170,16 @@
 MESH = pl.DeviceIdType.MESH
 CHUNKS = HEADS // 2 + 2
 WIDEN = 8
-PATHS = ("xzy", "zxy", "yzx", "xzy", "yxz", "xyz", "yzx", "yzx")
+PATHS = ("zxy", "yzx", "xyz", "yxz", "xyz", "yzx", "xzy", "yxz")
 ORDER = (
-    "osend", "back0", "pairs0", "back1", "pairs1", "fa10", "fa11", "last0", "pairs2", "last1", "fa01", "c2.1",
-    "pairs3", "fb1", "c4.1", "last2", "c5.1", "out1", "c3.1", "c2.2", "fa00", "out0", "finish0", "c6.1", "c1.1",
-    "c4.2", "c0.1", "c5.2", "finish1", "c3.2", "c7.1", "c6.2", "c2.3", "c1.2", "fb0", "c5.3", "fc", "c0.2", "c4.3",
-    "c5.4", "g1", "c1.3", "c6.3", "c2.4", "c3.3", "c7.2", "c0.3", "c4.4", "fd", "c1.4", "c5.5", "c0.4", "c4.5",
-    "c6.4", "c7.3", "c3.4", "c5.6", "g2", "c2.5", "c0.5", "c4.6", "c7.4", "c6.5", "fe", "c1.5", "c2.6", "c5.7",
-    "c3.5", "c4.7", "c0.6", "g3", "c6.6", "c7.5", "c3.6", "c2.7", "c1.6", "c0.7", "c7.6", "c5.8", "ff", "c6.7",
-    "c4.8", "o0", "c1.7", "g4", "c3.7", "c2.8", "c7.7", "c0.8", "c4.9", "c6.8", "c1.8", "c3.8", "c7.8", "c0.9",
-    "c5.9", "c1.9", "g5", "o1", "c6.9", "c2.9", "c3.9", "c7.9",
+    "back0", "osend", "pairs0", "back1", "pairs1", "fa11", "fa10", "fa01", "last0", "fa00", "out1", "pairs2", "out0",
+    "last1", "c3.1", "fb1", "c2.1", "pairs3", "c1.1", "last2", "c4.1", "finish0", "c5.1", "c0.1", "c2.2", "c3.2",
+    "c6.1", "finish1", "c1.2", "fb0", "c4.2", "c3.3", "c5.2", "c7.1", "c0.2", "g1", "c2.3", "c6.2", "c1.3", "fc",
+    "c4.3", "c3.4", "c0.3", "o0", "g2", "c2.4", "c7.2", "c6.3", "c5.3", "c1.4", "c4.4", "c3.5", "fd", "c0.4", "c6.4",
+    "c7.3", "c2.5", "c1.5", "c5.4", "c4.5", "c3.6", "g3", "c7.4", "c0.5", "o1", "c2.6", "c4.6", "g4", "c6.5", "c5.5",
+    "c1.6", "c0.6", "c7.5", "fe", "c3.7", "c2.7", "c5.6", "c6.6", "c1.7", "c0.7", "c7.6", "c4.7", "c5.7", "c3.8",
+    "c2.8", "c6.7", "c7.7", "c1.8", "c0.8", "c3.9", "c4.8", "g5", "c5.8", "c1.9", "c6.8", "c7.8", "ff", "c2.9",
+    "c6.9", "c5.9", "c4.9", "c0.9", "c7.9",
 )
 
 
@@ -471,7 +471,7 @@
         def _():
             gather_forward(0)
 
-        @pl.when(p == 5)
+        @pl.when(p == 4)
         def _():
             gather_forward(1)
 
@@ -732,6 +732,10 @@
             pltpu.make_async_copy(src.at[rows, :], dst.at[rows, :], store_sem.at[i, k]) for k, (src, dst) in enumerate(pairs)
         ]
 
+    for copy in passed:
+        copy.start()
+    g1_out[...], rw_out[...], g2_out[...] = small[0], small[1], small[2]
+
     @pl.loop(0, WIDEN)
     def _(i):
         rows = rows_of(i)
@@ -749,10 +753,6 @@
         f2_wide[rows, :] = gf2[core + c - 2 * core * c, inner, :].astype(F32)
         for copy in stores(i):
             copy.start()
-
-    for copy in passed:
-        copy.start()
-    g1_out[...], rw_out[...], g2_out[...] = small[0], small[1], small[2]
 
     @pl.loop(0, WIDEN)
     def _(i):

time: 127 us -> 126 us (level)
    pallas_call x1, Pallas kernels: 120 us -> 118 us  [per_device(): pl.pallas_call(mega_kernel, out_shape=[bf(patches, count, width), bf(patc...]
where the time goes in v2:
time: 126 us; the launch traced here: 125 us
  Pallas kernels  125 us (99%)
    pallas_call x1, Pallas kernels, per_device(): pl.pallas_call(mega_kernel, out_shape=[bf(patches, count, width), bf(patc...  118 us
    pallas_call x1, Pallas kernels, widen(): pl.pallas_call(widen_kernel, out_shape=[tokens, tokens] + [jax.ShapeDtype...  6.26 us

profile of v2, /device:TPU:0, one launch (start us, length us, event | category | flops | bytes accessed | tf_op | source)
XLA Modules:
  0.0 125.4 jit_solution(2566794304108555074)
XLA Ops:
  0.6 118.3 %block.1 = (bf16[197,2,768]{2,1,0:T(2,128)(2,1)S(1)}, bf16[197,2,768]{2,1,0:T(2,128)(2,1)S(1)}, bf16[8,768,384]{2,1,0:T(8,128)(2,1)S(1)}, bf16[2,768,384]{2,1,0:...) custom-call(bf16[197,2,768]{2,1,0:T(2,128)(2,1)} %bitcast.4, s32[2,197]{1,0:T(2,128)} %rank_hbm.1, ...), custom_call_target="tpu_custom_call" | custom-call | tf_op jit(solution)/shard_map/block/pallas_call | solution.py:818
  119.0 6.3 %widen.1 = (bf16[197,2,768]{2,1,0:T(2,128)(2,1)}, bf16[197,2,768]{2,1,0:T(2,128)(2,1)}, f32[768,2304]{1,0:T(8,128)}, f32[768,768]{1,0:T(8,128)}, f32[768,768]{1,...) custom-call(bf16[197,2,768]{2,1,0:T(2,128)(2,1)S(1)} %get-tuple-element.24.block, ...), custom_call_target="tpu_custom_call" | custom-call | tf_op jit(solution)/shard_map/widen/pallas_call | solution.py:770

commit v3 on v2

--- a/solution.py
+++ b/solution.py
@@ -397,13 +397,9 @@
         return remote(held, held, qs.at[j, step], qr.at[j, step], row, column)
 
     def chunk_step(j, step):
-        path = hops(j)
-        chunk_copy(j, step - 1).wait()
+        path, last = hops(j), chunk_copy(j, step - 1)
+        last.wait_recv()
         if step <= 4:
-            row, column, _ = path[step - 1]
-            pl.semaphore_signal(
-                chunk_free.at[j, step - 1], inc=1, device_id={"rows": row, "mlp": column}, device_id_type=MESH
-            )
             start = base(path, min(step, 4))
             if step < 4:
                 start = base(path, step) + (1 - path[step][2]) * sizes[step]
@@ -413,12 +409,20 @@
                 total = total + parts[level][j, ds(start - base(path, level + 1), size), :].astype(F32)
             gw[j, ds(start, size), :] = total.astype(BF)
         if step == 5:
+            last.wait_send()
             own = ds(base(path, 4), sizes[3])
             gw[j, own, :] = gw[j, own, :] + far[j]
         if 5 <= step <= 8:
             pl.semaphore_wait(chunk_free.at[j, 8 - step], 1)
         if step <= 8:
             chunk_copy(j, step).start()
+        if step != 5:
+            last.wait_send()
+        if step <= 4:
+            row, column, _ = path[step - 1]
+            pl.semaphore_signal(
+                chunk_free.at[j, step - 1], inc=1, device_id={"rows": row, "mlp": column}, device_id_type=MESH
+            )
 
     def small_copy(level):
         row = (r_sib, r_x, r_y)[level]

time: 126 us -> 126 us (level)
  no operation moved by 1% of the time
where the time goes in v3:
time: 126 us; the launch traced here: 125 us
  Pallas kernels  125 us (99%)
    pallas_call x1, Pallas kernels, per_device(): pl.pallas_call(mega_kernel, out_shape=[bf(patches, count, width), bf(patc...  118 us
    pallas_call x1, Pallas kernels, widen(): pl.pallas_call(widen_kernel, out_shape=[tokens, tokens] + [jax.ShapeDtype...  6.26 us

profile of v3, /device:TPU:0, one launch (start us, length us, event | category | flops | bytes accessed | tf_op | source)
XLA Modules:
  0.0 125.4 jit_solution(9680819277595156116)
XLA Ops:
  0.6 118.3 %block.1 = (bf16[197,2,768]{2,1,0:T(2,128)(2,1)S(1)}, bf16[197,2,768]{2,1,0:T(2,128)(2,1)S(1)}, bf16[8,768,384]{2,1,0:T(8,128)(2,1)S(1)}, bf16[2,768,384]{2,1,0:...) custom-call(bf16[197,2,768]{2,1,0:T(2,128)(2,1)} %bitcast.4, s32[2,197]{1,0:T(2,128)} %rank_hbm.1, ...), custom_call_target="tpu_custom_call" | custom-call | tf_op jit(solution)/shard_map/block/pallas_call | solution.py:822
  119.0 6.3 %widen.1 = (bf16[197,2,768]{2,1,0:T(2,128)(2,1)}, bf16[197,2,768]{2,1,0:T(2,128)(2,1)}, f32[768,2304]{1,0:T(8,128)}, f32[768,768]{1,0:T(8,128)}, f32[768,768]{1,...) custom-call(bf16[197,2,768]{2,1,0:T(2,128)(2,1)S(1)} %get-tuple-element.24.block, ...), custom_call_target="tpu_custom_call" | custom-call | tf_op jit(solution)/shard_map/widen/pallas_call | solution.py:774

commit v4 on v3

--- a/solution.py
+++ b/solution.py
@@ -471,11 +471,11 @@
         for i in range(images):
             attend(p, i, width, tall, qkv, keep, probs, context, contextt)
 
-        @pl.when(p == 2)
+        @pl.when(p == 0)
         def _():
             gather_forward(0)
 
-        @pl.when(p == 4)
+        @pl.when(p == 3)
         def _():
             gather_forward(1)
 
@@ -519,7 +519,6 @@
     def before_near():
         cot_copy(2).wait_recv()
         gh2_to_sib.start()
-        out_to_sib.start()
 
     def forward_token(i):
         token_copy(i, 1).wait_recv()
@@ -572,6 +571,7 @@
         at(block, 5, lambda: gh2_over(0).start())
         at(block, 7, lambda: gh2_over(1).start())
 
+    out_to_sib.start()
     out_over.start()
     turned[...] = tok[...].T
     for m in range(3):

time: 126 us -> 126 us (level)
  no operation moved by 1% of the time
where the time goes in v4:
time: 126 us; the launch traced here: 125 us
  Pallas kernels  125 us (99%)
    pallas_call x1, Pallas kernels, per_device(): pl.pallas_call(mega_kernel, out_shape=[bf(patches, count, width), bf(patc...  118 us
    pallas_call x1, Pallas kernels, widen(): pl.pallas_call(widen_kernel, out_shape=[tokens, tokens] + [jax.ShapeDtype...  6.26 us

profile of v4, /device:TPU:0, one launch (start us, length us, event | category | flops | bytes accessed | tf_op | source)
XLA Modules:
  0.0 125.4 jit_solution(5381023639926237809)
XLA Ops:
  0.6 118.3 %block.1 = (bf16[197,2,768]{2,1,0:T(2,128)(2,1)S(1)}, bf16[197,2,768]{2,1,0:T(2,128)(2,1)S(1)}, bf16[8,768,384]{2,1,0:T(8,128)(2,1)S(1)}, bf16[2,768,384]{2,1,0:...) custom-call(bf16[197,2,768]{2,1,0:T(2,128)(2,1)} %bitcast.4, s32[2,197]{1,0:T(2,128)} %rank_hbm.1, ...), custom_call_target="tpu_custom_call" | custom-call | tf_op jit(solution)/shard_map/block/pallas_call | solution.py:822
  119.0 6.3 %widen.1 = (bf16[197,2,768]{2,1,0:T(2,128)(2,1)}, bf16[197,2,768]{2,1,0:T(2,128)(2,1)}, f32[768,2304]{1,0:T(8,128)}, f32[768,768]{1,0:T(8,128)}, f32[768,768]{1,...) custom-call(bf16[197,2,768]{2,1,0:T(2,128)(2,1)S(1)} %get-tuple-element.24.block, ...), custom_call_target="tpu_custom_call" | custom-call | tf_op jit(solution)/shard_map/widen/pallas_call | solution.py:774

commit v5 on v3

--- a/solution.py
+++ b/solution.py
@@ -169,7 +169,7 @@
 
 MESH = pl.DeviceIdType.MESH
 CHUNKS = HEADS // 2 + 2
-WIDEN = 8
+WIDEN = 16
 PATHS = ("zxy", "yzx", "xyz", "yxz", "xyz", "yzx", "xzy", "yxz")
 ORDER = (
     "back0", "osend", "pairs0", "back1", "pairs1", "fa11", "fa10", "fa01", "last0", "fa00", "out1", "pairs2", "out0",

time: 126 us -> 126 us (level)
  no operation moved by 1% of the time
where the time goes in v5:
time: 126 us
  Pallas kernels  125 us (99%)
    pallas_call x1, Pallas kernels, per_device(): pl.pallas_call(mega_kernel, out_shape=[bf(patches, count, width), bf(patc...  118 us
    pallas_call x1, Pallas kernels, widen(): pl.pallas_call(widen_kernel, out_shape=[tokens, tokens] + [jax.ShapeDtype...  6.53 us

profile of v5, /device:TPU:0, one launch (start us, length us, event | category | flops | bytes accessed | tf_op | source)
XLA Modules:
  0.0 125.7 jit_solution(17200642984748679226)
XLA Ops:
  0.6 118.3 %block.1 = (bf16[197,2,768]{2,1,0:T(2,128)(2,1)S(1)}, bf16[197,2,768]{2,1,0:T(2,128)(2,1)S(1)}, bf16[8,768,384]{2,1,0:T(8,128)(2,1)S(1)}, bf16[2,768,384]{2,1,0:...) custom-call(bf16[197,2,768]{2,1,0:T(2,128)(2,1)} %bitcast.4, s32[2,197]{1,0:T(2,128)} %rank_hbm.1, ...), custom_call_target="tpu_custom_call" | custom-call | tf_op jit(solution)/shard_map/block/pallas_call | solution.py:822
  119.0 6.5 %widen.1 = (bf16[197,2,768]{2,1,0:T(2,128)(2,1)}, bf16[197,2,768]{2,1,0:T(2,128)(2,1)}, f32[768,2304]{1,0:T(8,128)}, f32[768,768]{1,0:T(8,128)}, f32[768,768]{1,...) custom-call(bf16[197,2,768]{2,1,0:T(2,128)(2,1)S(1)} %get-tuple-element.24.block, ...), custom_call_target="tpu_custom_call" | custom-call | tf_op jit(solution)/shard_map/widen/pallas_call | solution.py:774
